TPU v7x, 32 devices: a whole 2x2x4 slice. The times are simulated.
32 devices in a mesh: dp: 4 (over z), space: 8 (over y, x, core).
Axes of the slice: x: 2, y: 2, z: 4, core: 2. Of those that a mesh axis runs over, the one named last changes fastest.
Arguments:
- activations: bfloat16 [4, 16, 180, 768], P('dp', 'space'), may hold values from -6 to 6
- cotangent: bfloat16 [4, 16, 180, 768], P('dp', 'space'), may hold values from -6 to 6
- w_first: bfloat16 [2, 768, 96], replicated, may hold values from -0.4375 to 0.4375
- w_second: bfloat16 [2, 768, 96], replicated, may hold values from -0.4375 to 0.4375
- b_first: float32 [2, 768], replicated, may hold values from -3 to 3
- lon_keep: int32 [8], replicated, may hold values from 0 to 90, as said below
- relu_mask: int32 [4, 16, 2, 8, 768], P('dp', None, None, 'space'), may hold values 0 or 1
- shrink_mask: int32 [4, 16, 2, 8, 768], P('dp', None, None, 'space'), may hold values 0 or 1
Outputs:
- grad_activations: bfloat16 [4, 16, 180, 768], P('dp', 'space')
- grad_w_first: float32 [2, 768, 96], P(None, 'dp')
- grad_w_second: float32 [2, 768, 96], P(None, 'dp')
- grad_b_first: float32 [2, 768], P(None, 'dp')
- grad_b_second: float32 [2, 768], P(None, 'dp')
Inputs may be any that keep to these rules, and one draw needn't show every extreme that they name: `lon_keep`: 8 distinct longitude frequencies, 0 and 90 among them, in no particular order.
All inputs are finite; a program needn't handle non-finite values. No bound on the sum of `relu_mask` or of `shrink_mask` on one device may be relied on, other than what follows from the above.
Results may differ from a plain program's by a relative error of at most 0.011.
Values may be sent and summed in bfloat16 or wider, within the bound.
No kernel may reach another device: no remote copies, remote signals or barrier semaphores. Data moves between devices by JAX's collectives and lax.ppermute only.
A program may use at most 64 MiB of HBM per device.

v0:
```python
import functools
import math

import jax
import jax.numpy as jnp
import numpy as np
from jax import lax
from jax.experimental import pallas as pl
from jax.experimental.pallas import tpu as pltpu
from jax.sharding import PartitionSpec as P

C = 768
BLOCKS = 8
LON = 180
BS = 96

BF = jnp.bfloat16
F32 = jnp.float32
LANES = 128
THIRD = LANES - BS
VMEM_LIMIT = 32 * 1024 * 1024


def shift_of(group):
    return 2 * (group % 2) + group // 2


def block_of(group, device):
    lane = 2 * (device // 4) + device % 2
    return 2 * ((lane + shift_of(group)) % 4) + (device // 2) % 2


def owner_of(group, block):
    lane = (block // 2 + 4 - shift_of(group)) % 4
    return 4 * (lane // 2) + 2 * (block % 2) + lane % 2


def latitude_matrix(lat_len, kept):
    index = np.arange(lat_len)
    angle = ((index[:, None] * index[None, :]) % lat_len).astype(np.float32) * np.float32(
        2.0 * math.pi / lat_len
    )
    cosine, sine = np.cos(angle), np.sin(angle)
    table = np.stack([np.stack([cosine, sine], -1), np.stack([-sine, cosine], -1)], 1)
    full = np.einsum("mphq,jk->pjmhqk", table, np.eye(kept, dtype=np.float32))
    return full.reshape(2 * kept * lat_len, 2 * kept * lat_len)


def dot(lhs, rhs, lhs_axis, rhs_axis):
    return lax.dot_general(
        lhs, rhs, (((lhs_axis,), (rhs_axis,)), ((), ())), preferred_element_type=F32
    )


def fold(array):
    rows = array.shape[0] // 4
    beside = [array[3 * rows :, g * THIRD : (g + 1) * THIRD] for g in range(3)]
    return jnp.concatenate([array[: 3 * rows], jnp.concatenate(beside, axis=0)], axis=1)


def unfold(array):
    rows = array.shape[0] // 3
    beside = [array[g * rows : (g + 1) * rows, BS:] for g in range(3)]
    return jnp.concatenate([array[:, :BS], jnp.concatenate(beside, axis=1)], axis=0)


def window_of(block):
    tile = jnp.minimum(block * BS // LANES, C // LANES - 2)
    return pl.multiple_of(tile * LANES, LANES), block * BS - tile * LANES


def forward_lon_kernel(
    keep_hbm,
    act_hbm,
    cot_hbm,
    relu_hbm,
    shrink_hbm,
    *refs,
):
    weights_hbm, matrices_hbm, refs = refs[:3], refs[3:5], refs[5:]
    out, table_out, *fetched, field, masks, keep, sems = refs
    group, device = lax.axis_index("dp"), lax.axis_index("space")
    start, _ = window_of(block_of(group, device))
    kept = keep.shape[0]
    rows = act_hbm.shape[1]
    modes = relu_hbm.shape[0]
    tiles = C // LANES
    columns = [slice(k * LANES, (k + 1) * LANES) for k in range(tiles)]
    keep_copy = pltpu.make_async_copy(keep_hbm, keep, sems.at[0])
    keep_copy.start()
    mask_copies, field_copies = [], []
    for t, source in enumerate((relu_hbm, shrink_hbm)):
        for p in range(2):
            for k in range(tiles):
                copy = pltpu.make_async_copy(
                    source.at[:, p, :, columns[k]],
                    masks.at[t, p, k],
                    sems.at[1 + (2 * t + p) * tiles + k],
                )
                copy.start()
                mask_copies.append(copy)
    for t, source in enumerate((act_hbm, cot_hbm)):
        for k in range(tiles):
            copy = pltpu.make_async_copy(
                source.at[:, :, columns[k]], field.at[t, k], sems.at[1 + (4 + t) * tiles + k]
            )
            copy.start()
            field_copies.append(copy)
    sources = [
        source.at[(slice(None),) * (len(source.shape) - 1) + (pl.ds(start, 2 * LANES),)]
        for source in weights_hbm
    ] + list(matrices_hbm)
    other_copies = []
    for i, (source, target) in enumerate(zip(sources, fetched)):
        copy = pltpu.make_async_copy(source, target, sems.at[1 + 6 * tiles + i])
        copy.start()
        other_copies.append(copy)

    keep_copy.wait()
    shape = (rows * 2 * kept, LON * rows)
    line = lax.broadcasted_iota(jnp.int32, shape, 0)
    column = lax.broadcasted_iota(jnp.int32, shape, 1)
    frequency = jnp.zeros(shape, jnp.int32)
    for j in range(kept):
        frequency = jnp.where(line % kept == j, keep[j], frequency)
    turn = jnp.where((line // kept) % 2 == 1, LON // 4, 0)
    phase = ((column // rows) * frequency + turn) % LON
    table = jnp.cos(phase.astype(F32) * (2.0 * math.pi / LON))
    wide_table = jnp.where(line // (2 * kept) == column % rows, table, 0.0)
    table = wide_table.astype(BF)
    table_out[...] = wide_table.T.astype(BF)

    own = keep[device]
    scale = jnp.where((own == 0) | (2 * own == LON), 1.0, 2.0)
    for copy in mask_copies:
        copy.wait()

    def gate(t, value):
        return jnp.concatenate(
            [
                jnp.concatenate(
                    [
                        jnp.where(masks.at[t, p, k].reshape(modes, LANES)[...] > 0, value, 0.0)
                        for k in range(tiles)
                    ],
                    axis=1,
                )
                for p in range(2)
            ],
            axis=0,
        ).astype(BF)

    passed = gate(0, 1.0)
    scaled = gate(1, scale)
    per = table.shape[0]
    owners = [owner_of(group, b) for b in range(BLOCKS)]
    for b in range(BLOCKS):
        out[owners[b], 2 * per :, 0:BS] = passed[:, b * BS : (b + 1) * BS]
        beside = [scaled[:, b * BS + g * THIRD : b * BS + (g + 1) * THIRD] for g in range(3)]
        out[owners[b], :, BS:] = jnp.concatenate(beside, axis=0)

    for t in range(2):
        for copy in field_copies[t * tiles : (t + 1) * tiles]:
            copy.wait()
        wide = jnp.concatenate(
            [
                field[t, k].reshape(LON * rows, LANES) for k in range(tiles)
            ],
            axis=1,
        )
        lines = dot(table, wide, 1, 0).astype(BF)
        for b in range(BLOCKS):
            out[owners[b], t * per : (t + 1) * per, 0:BS] = lines[:, b * BS : (b + 1) * BS]
    for copy in other_copies:
        copy.wait()


def block_adjoint(operand, matrix):
    half = operand.shape[0] // 2
    real = dot(operand, matrix[0], 1, 0)
    imag = dot(operand, matrix[1], 1, 0)
    return jnp.concatenate([real[:half] + imag[half:], real[half:] - imag[:half]], axis=0)


def spectral_kernel(
    pieces, first_wide, second_wide, bias_wide, lat, terms, grad_pre_out, first_out, *, ortho_scale, rows, kept
):
    device = lax.axis_index("space")
    _, offset = window_of(block_of(lax.axis_index("dp"), device))
    parts = pieces.shape[0]
    per = rows * 2 * kept
    half = parts * per // 2
    modes = half // kept
    chosen = lax.broadcasted_iota(jnp.int32, (2 * LANES, BS), 0) == (
        lax.broadcasted_iota(jnp.int32, (2 * LANES, BS), 1) + offset
    )
    chosen = jnp.where(chosen, 1.0, 0.0).astype(BF)
    first = [dot(first_wide[p], chosen, 1, 0).astype(BF) for p in range(2)]
    second = [dot(second_wide[p], chosen, 1, 0).astype(BF) for p in range(2)]
    bias = pltpu.roll(bias_wide[...], (2 * LANES - offset) % (2 * LANES), 1)
    opened = [unfold(pieces[i]) for i in range(parts)]

    def spectrum(t):
        stacked = jnp.concatenate([piece[t * per : (t + 1) * per] for piece in opened], axis=0)
        return (dot(lat[...], stacked, 1, 0) * ortho_scale).astype(BF)

    def mask(k):
        start = 2 * per + k * 2 * modes
        return jnp.concatenate(
            [
                opened[j][start + p * modes : start + (p + 1) * modes]
                for p in range(2)
                for j in range(kept)
            ],
            axis=0,
        ).astype(F32)

    spec_act = spectrum(0)
    spec_cot = spectrum(1)
    passed = mask(0) > 0.0
    weight = mask(1)
    grad_out = jnp.where(weight > 0.0, weight * spec_cot.astype(F32), 0.0).astype(BF)

    by_real = dot(spec_act, first[0], 1, 1)
    by_imag = dot(spec_act, first[1], 1, 1)
    pre = jnp.concatenate(
        [
            by_real[:half] - by_imag[half:] + bias[0:1, :BS],
            by_imag[:half] + by_real[half:] + bias[1:2, :BS],
        ],
        axis=0,
    )
    hidden = jnp.where(passed, pre, 0.0).astype(BF)

    grad_pre = jnp.where(passed, block_adjoint(grad_out, second), 0.0).astype(BF)
    grad_pre_out[...] = grad_pre
    for p in range(2):
        first_out[p] = first[p]

    def turned(array):
        return jnp.concatenate([array[half:], -array[:half]], axis=0)

    at = 3 * BS // 4
    blank = jnp.zeros((terms.shape[2] - at - 1, LANES), F32)
    for a, (left, right) in enumerate(((spec_act, grad_pre), (hidden, grad_out))):
        slot = (a + device) % 2
        wide = right.astype(F32)
        for p, other in enumerate((right, turned(right))):
            summed = jnp.sum(wide[p * half : (p + 1) * half], axis=0, keepdims=True)
            summed = jnp.concatenate([summed, jnp.zeros((1, THIRD), F32)], axis=1)
            terms[slot, p] = jnp.concatenate(
                [fold(dot(left, other, 0, 0)), summed, blank], axis=0
            ).astype(BF)


def grad_lat_kernel(grad_pre, first, lat_t, grad_lat):
    grad_spec = block_adjoint(grad_pre[...], first).astype(BF)
    lines = dot(lat_t[...], grad_spec, 1, 0)
    lines = jnp.concatenate([lines, jnp.zeros((lines.shape[0], THIRD), F32)], axis=1).astype(BF)
    grad_lat[...] = lines.reshape(grad_lat.shape)


def inverse_lon_kernel(table, pieces, field, *, ortho_scale):
    rows = field.shape[1]
    per = table.shape[1]
    group = lax.axis_index("dp")
    lines = jnp.concatenate(
        [pieces[owner_of(group, b), 0:per, 0:BS] for b in range(BLOCKS)], axis=1
    )
    wide = (dot(table[...], lines, 1, 0) * ortho_scale).astype(BF)
    for k in range(C // LANES):
        lanes = slice(k * LANES, (k + 1) * LANES)
        field[:, :, lanes] = wide[:, lanes].reshape(LON, rows, LANES)


def gathered_kernel(pieces, others, first, second, bias_first, bias_second, *, grad_norm):
    core = lax.axis_index("space") % 2
    per = pieces.shape[1] - others.shape[1]
    at = 3 * BS // 4
    for a, (target, vector) in enumerate(((first, bias_first), (second, bias_second))):
        for k in range(2):
            near, far = 2 * k + a, 4 + 2 * k + a
            own = pieces[near, per:, :].astype(F32) + pieces[far, per:, :].astype(F32)
            other = others[near].astype(F32) + others[far].astype(F32)
            for p in range(2):
                total = jnp.where(core == p, own, other) * grad_norm
                target[p, k * BS : (k + 1) * BS, :] = unfold(total[:at])
                vector[p : p + 1, k * BS : (k + 1) * BS] = total[at : at + 1, :BS]


def whole(memory=pltpu.VMEM):
    return pl.BlockSpec(memory_space=memory)


def by_blocks(
    activations, cotangent, w_first, w_second, b_first, lon_keep, relu_mask, shrink_mask
):
    groups = lax.axis_size("dp")
    parts = lax.axis_size("space")
    rows = activations.shape[1]
    lat_len = rows * parts
    kept = lon_keep.shape[0]
    ortho_scale = 1.0 / math.sqrt(lat_len * LON)
    grad_norm = 1.0 / math.sqrt(groups * lat_len * kept)
    params = pltpu.CompilerParams(vmem_limit_bytes=VMEM_LIMIT)
    tiles = C // LANES
    per = rows * 2 * kept
    height = (2 * per + 4 * lat_len) * 3 // 4
    term_rows = 3 * BS // 4 + 8

    lat = latitude_matrix(lat_len, kept)
    sent, table, *fetched = pl.pallas_call(
        forward_lon_kernel,
        out_shape=(
            pltpu.VMEM((parts, height, LANES), BF),
            pltpu.VMEM((LON * rows, per), BF),
            pltpu.VMEM((2, BS, 2 * LANES), BF),
            pltpu.VMEM((2, BS, 2 * LANES), BF),
            pltpu.VMEM((2, 2 * LANES), F32),
            pltpu.VMEM(lat.shape, BF),
            pltpu.VMEM(lat.shape, BF),
        ),
        in_specs=[whole(pl.ANY)] * 10,
        out_specs=(whole(),) * 7,
        scratch_shapes=[
            pltpu.VMEM((2, tiles, LON, rows, LANES), BF),
            pltpu.VMEM((2, 2, tiles, lat_len, 1, LANES), jnp.int32),
            pltpu.SMEM((kept,), jnp.int32),
            pltpu.SemaphoreType.DMA((6 + 6 * tiles,)),
        ],
        compiler_params=params,
        name="forward_lon",
    )(
        *(
            pltpu.with_memory_space_constraint(array, pltpu.HBM)
            for array in (
                lon_keep,
                activations[0].transpose(1, 0, 2),
                cotangent[0].transpose(1, 0, 2),
                relu_mask[0],
                shrink_mask[0],
                w_first.transpose(0, 2, 1),
                w_second.transpose(0, 2, 1),
                b_first,
                jnp.asarray(lat, BF),
                jnp.asarray(lat.T, BF),
            )
        )
    )
    pieces = lax.all_to_all(sent, "space", 0, 0, tiled=True)

    *fetched, lat_t = fetched
    terms, grad_pre, first_block = pl.pallas_call(
        functools.partial(spectral_kernel, ortho_scale=ortho_scale, rows=rows, kept=kept),
        out_shape=(
            jax.ShapeDtypeStruct((2, 2, term_rows, LANES), BF),
            pltpu.VMEM((lat.shape[0], BS), BF),
            pltpu.VMEM((2, BS, BS), BF),
        ),
        in_specs=[whole()] * 5,
        out_specs=(whole(),) * 3,
        compiler_params=params,
        name="spectral",
    )(pieces, *fetched)
    grad_lat = pl.pallas_call(
        grad_lat_kernel,
        out_shape=jax.ShapeDtypeStruct((parts, per, LANES), BF),
        in_specs=[whole()] * 3,
        out_specs=whole(),
        compiler_params=params,
        cost_estimate=pl.CostEstimate(
            flops=2 * lat.size * BS * 3, bytes_accessed=4 * lat.size, transcendentals=0
        ),
        name="grad_lat",
    )(grad_pre, first_block, lat_t)

    arrived = lax.ppermute(
        terms,
        ("dp", "space"),
        [
            (g * parts + c, (block_of(g, c) // 2) * parts + c)
            for g in range(groups)
            for c in range(parts)
        ],
    )
    other = lax.ppermute(arrived[1], "space", [(c, c ^ 1) for c in range(parts)])
    share = (arrived[0].astype(F32) + other.astype(F32)).astype(BF)
    share = jnp.broadcast_to(share[None], (parts // 2,) + share.shape)
    returned = lax.all_to_all(
        jnp.concatenate([grad_lat, share.reshape(parts, term_rows, LANES)], axis=1),
        "space",
        0,
        0,
        tiled=True,
    )
    others = lax.ppermute(returned[:, per:, :], "space", [(c, c ^ 1) for c in range(parts)])

    keep_rows = C // groups
    field = pl.pallas_call(
        functools.partial(inverse_lon_kernel, ortho_scale=ortho_scale),
        out_shape=jax.ShapeDtypeStruct((LON, rows, C), BF),
        in_specs=[whole(), whole()],
        out_specs=whole(),
        compiler_params=params,
        cost_estimate=pl.CostEstimate(
            flops=2 * per * LON * rows * C, bytes_accessed=8 * LON * rows * C, transcendentals=0
        ),
        name="inverse_lon",
    )(table, returned)
    first, second, bias_first, bias_second = pl.pallas_call(
        functools.partial(gathered_kernel, grad_norm=grad_norm),
        out_shape=(
            jax.ShapeDtypeStruct((2, keep_rows, BS), F32),
            jax.ShapeDtypeStruct((2, keep_rows, BS), F32),
            jax.ShapeDtypeStruct((2, keep_rows), F32),
            jax.ShapeDtypeStruct((2, keep_rows), F32),
        ),
        in_specs=[whole(), whole()],
        out_specs=(whole(),) * 4,
        compiler_params=params,
        name="gathered",
    )(returned, others)
    return field.transpose(1, 0, 2)[None], first, second, bias_first, bias_second


def build_tables(lon_keep, lat_len, lon_len):
    columns = jnp.arange(lon_len, dtype=jnp.int32)
    lon_phase = columns[:, None] * lon_keep[None, :] % lon_len
    lon_angle = lon_phase.astype(jnp.float32) * (2.0 * math.pi / lon_len)
    lon_table = jnp.stack([jnp.cos(lon_angle), -jnp.sin(lon_angle)], axis=1).astype(jnp.bfloat16)
    latitudes = jnp.arange(lat_len, dtype=jnp.int32)
    lat_phase = latitudes[:, None] * latitudes[None, :] % lat_len
    lat_angle = lat_phase.astype(jnp.float32) * (2.0 * math.pi / lat_len)
    cosine = jnp.cos(lat_angle)
    sine_part = jnp.sin(lat_angle)
    lat_table = jnp.stack(
        [jnp.stack([cosine, sine_part], axis=-1), jnp.stack([-sine_part, cosine], axis=-1)], axis=1
    ).astype(jnp.bfloat16)
    return (lon_table, lat_table)


def apply_blocks(operand, matrix):
    return jnp.einsum("smjbc,bcd->smjbd", operand, matrix, preferred_element_type=jnp.float32)


def adjoint(operand, matrix):
    return jnp.einsum("smjbd,bcd->smjbc", operand, matrix, preferred_element_type=jnp.float32)


def outer_sum(operand, other):
    return jnp.einsum("smjbc,smjbd->bcd", operand, other, preferred_element_type=jnp.float32)


def by_frequencies(
    activations, cotangent, w_first, w_second, b_first, lon_keep, relu_mask, shrink_mask
):
    parts = lax.axis_size("space")
    samples_dev = activations.shape[0]
    lat_len = activations.shape[1] * parts
    kept = lon_keep.shape[0]
    owned = kept // parts
    lon_table, lat_table = build_tables(lon_keep, lat_len, LON)
    ortho_scale = 1.0 / math.sqrt(lat_len * LON)
    act_lon = jnp.einsum(
        "shwc,wpk->shpkc", activations, lon_table, preferred_element_type=jnp.float32
    ).astype(jnp.bfloat16)
    cot_lon = jnp.einsum(
        "shwc,wpk->shpkc", cotangent, lon_table, preferred_element_type=jnp.float32
    ).astype(jnp.bfloat16)
    act_modes, cot_modes = (
        lax.all_to_all(act_lon, "space", split_axis=3, concat_axis=1, tiled=True),
        lax.all_to_all(cot_lon, "space", split_axis=3, concat_axis=1, tiled=True),
    )

    def latitude(modes):
        summed = jnp.einsum(
            "mphq,shqjc->smpjc", lat_table, modes, preferred_element_type=jnp.float32
        )
        return (summed * ortho_scale).astype(jnp.bfloat16)

    block_shape = (samples_dev, lat_len, 2, owned, BLOCKS, BS)
    spec_act = latitude(act_modes).reshape(block_shape)
    spec_cot = latitude(cot_modes)
    own_keep = lax.dynamic_slice_in_dim(lon_keep, lax.axis_index("space") * owned, owned)
    doubled = jnp.where((own_keep == 0) | (2 * own_keep == LON), 1.0, 2.0).astype(jnp.float32)
    grad_out = (
        jnp.where(
            shrink_mask > 0, doubled[None, None, None, :, None] * spec_cot.astype(jnp.float32), 0.0
        )
        .astype(jnp.bfloat16)
        .reshape(block_shape)
    )
    relu_gate = relu_mask.reshape(block_shape) > 0
    first_blocks = w_first.reshape(2, BLOCKS, BS, BS)
    second_blocks = w_second.reshape(2, BLOCKS, BS, BS)
    bias_blocks = b_first.reshape(2, BLOCKS, BS)
    act_real = spec_act[:, :, 0]
    act_imag = spec_act[:, :, 1]
    pre_real = (
        apply_blocks(act_real, first_blocks[0])
        - apply_blocks(act_imag, first_blocks[1])
        + bias_blocks[0]
    )
    pre_imag = (
        apply_blocks(act_real, first_blocks[1])
        + apply_blocks(act_imag, first_blocks[0])
        + bias_blocks[1]
    )
    hidden = jnp.where(relu_gate, jnp.stack([pre_real, pre_imag], axis=2), 0.0).astype(jnp.bfloat16)
    out_real = grad_out[:, :, 0]
    out_imag = grad_out[:, :, 1]
    hidden_real = adjoint(out_real, second_blocks[0]) + adjoint(out_imag, second_blocks[1])
    hidden_imag = -adjoint(out_real, second_blocks[1]) + adjoint(out_imag, second_blocks[0])
    grad_pre = jnp.where(relu_gate, jnp.stack([hidden_real, hidden_imag], axis=2), 0.0).astype(
        jnp.bfloat16
    )
    pre_grad_real = grad_pre[:, :, 0]
    pre_grad_imag = grad_pre[:, :, 1]
    spec_real = adjoint(pre_grad_real, first_blocks[0]) + adjoint(pre_grad_imag, first_blocks[1])
    spec_imag = -adjoint(pre_grad_real, first_blocks[1]) + adjoint(pre_grad_imag, first_blocks[0])
    grad_spec = (
        jnp.stack([spec_real, spec_imag], axis=2)
        .astype(jnp.bfloat16)
        .reshape(samples_dev, lat_len, 2, owned, C)
    )
    first_grad = jnp.stack(
        [
            outer_sum(act_real, pre_grad_real) + outer_sum(act_imag, pre_grad_imag),
            outer_sum(act_real, pre_grad_imag) - outer_sum(act_imag, pre_grad_real),
        ]
    ).reshape(2, C, BS)
    hid_real = hidden[:, :, 0]
    hid_imag = hidden[:, :, 1]
    second_grad = jnp.stack(
        [
            outer_sum(hid_real, out_real) + outer_sum(hid_imag, out_imag),
            outer_sum(hid_real, out_imag) - outer_sum(hid_imag, out_real),
        ]
    ).reshape(2, C, BS)
    bias_first = jnp.sum(grad_pre, axis=(0, 1, 3), dtype=jnp.float32).reshape(2, C)
    bias_second = jnp.sum(grad_out, axis=(0, 1, 3), dtype=jnp.float32).reshape(2, C)
    local_terms = (first_grad, second_grad, bias_first, bias_second)
    summed = lax.psum(
        (local_terms[0], local_terms[1], local_terms[2], local_terms[3]), ("dp", "space")
    )
    share_rows = C // lax.axis_size("dp")
    row_start = lax.axis_index("dp") * share_rows

    def take_share(array):
        return lax.dynamic_slice_in_dim(array, row_start, share_rows, 1)

    totals = jax.tree.map(take_share, summed)
    grad_norm = 1.0 / math.sqrt(samples_dev * lax.axis_size("dp") * lat_len * kept)
    grad_lat = jnp.einsum(
        "mqhp,smqjc->shpjc", lat_table, grad_spec, preferred_element_type=jnp.float32
    ).astype(jnp.bfloat16)
    returned = lax.all_to_all(grad_lat, "space", split_axis=1, concat_axis=3, tiled=True)
    grad_field = (
        jnp.einsum("wpk,shpkc->shwc", lon_table, returned, preferred_element_type=jnp.float32)
        * ortho_scale
    ).astype(jnp.bfloat16)
    return (
        grad_field,
        totals[0] * grad_norm,
        totals[1] * grad_norm,
        totals[2] * grad_norm,
        totals[3] * grad_norm,
    )


def solution(mesh):
    groups, parts = mesh.shape["dp"], mesh.shape["space"]

    def per_device(*arrays):
        activations, lon_keep = arrays[0], arrays[5]
        fits = (
            parts == BLOCKS
            and 2 * groups == BLOCKS
            and activations.shape[:2] == (1, 2)
            and lon_keep.shape[0] == parts
        )
        return by_blocks(*arrays) if fits else by_frequencies(*arrays)

    return jax.shard_map(
        per_device,
        mesh=mesh,
        in_specs=(
            P("dp", "space", None, None),
            P("dp", "space", None, None),
            P(),
            P(),
            P(),
            P(),
            P("dp", None, None, "space", None),
            P("dp", None, None, "space", None),
        ),
        out_specs=(
            P("dp", "space", None, None),
            P(None, "dp", None),
            P(None, "dp", None),
            P(None, "dp"),
            P(None, "dp"),
        ),
        check_vma=False,
    )
```

profile of v0, /device:TPU:0, one launch (start us, length us, event | category | flops | bytes accessed | tf_op | source)
XLA Modules:
  0.0 34.2 jit_solution(3203195991574859415)
XLA Ops:
  0.6 2.6 %forward_lon.1 = (bf16[8,96,128]{2,1,0:T(8,128)(2,1)S(1)}, bf16[360,32]{1,0:T(8,128)(2,1)S(1)}, bf16[2,96,256]{2,1,0:T(8,128)(2,1)S(1)}, bf16[2,96,256]{2,1,0:T(...) custom-call(s32[8]{0:T(128)} %keep_hbm.1, ...), custom_call_target="tpu_custom_call" | custom-call | tf_op jit(solution)/shard_map/forward_lon/pallas_call | solution.py:312
  3.2 11.2 %all_to_all.10.pieces = bf16[8,96,128]{2,1,0:T(8,128)(2,1)S(1)} all-to-all(bf16[8,96,128]{2,1,0:T(8,128)(2,1)S(1)} %get-tuple-element.20), channel_id=1, replica_groups=mesh['dp'=4,'space'=8] {'space'}, dimensions={0} | all-to-all | bytes 393216 | tf_op jit(solution)/shard_map/all_to_all | solution.py:350
  14.4 0.8 %spectral.1 = (bf16[2,2,80,128]{3,2,1,0:T(8,128)(2,1)S(1)}, bf16[256,96]{1,0:T(8,128)(2,1)S(1)}, bf16[2,96,96]{2,1,0:T(8,128)(2,1)S(1)}) custom-call(bf16[8,96,128]{2,1,0:T(8,128)(2,1)S(1)} %all_to_all.10.pieces, bf16[2,96,256]{2,1,0:T(8,128)(2,1)S(1)} %get-tuple-element.21.first_wide, bf16[2,96,256]{2,1,0:T(8,128)(2,1)S(1)} %get-tuple-element.22.second_wide, ...), custom_call_target="tpu_custom_call" | custom-call | tf_op jit(solution)/shard_map/spectral/pallas_call | solution.py:353
  15.3 0.7 %collective-permute-start = (bf16[2,2,80,128]{3,2,1,0:T(8,128)(2,1)S(1)}, bf16[2,2,80,128]{3,2,1,0:T(8,128)(2,1)S(1)}, u32[]{:S(2)}, u32[]{:S(2)}) collective-permute-start(bf16[2,2,80,128]{3,2,1,0:T(8,128)(2,1)S(1)} %get-tuple-element.28), channel_id=1, source_target_pairs={{0,0},{1,9},{2,2},{3,11},{4,20},{5,29},{6,22},{7,31},{8,16},{9,25}... | collective-permute-start | bytes 245768 | tf_op jit(solution)/shard_map/ppermute | solution.py:377
  15.9 0.0 collective-permute-done
  15.9 5.9 %collective-permute-start.1 = (bf16[2,80,128]{2,1,0:T(8,128)(2,1)S(1)}, bf16[2,80,128]{2,1,0:T(8,128)(2,1)S(1)}, u32[]{:S(2)}, u32[]{:S(2)}) collective-permute-start(bf16[2,80,128]{2,1,0:T(8,128)(2,1)S(1)} %slice_bitcast_fusion), channel_id=1, source_target_pairs={{0,1},{1,0},{2,3},{3,2},{4,5},{5,4},{6,7},{7,6},{8,9},{9,8},{10,11... | collective-permute-start | bytes 122888 | tf_op jit(solution)/shard_map/ppermute | solution.py:386
  21.9 0.4 %grad_lat.1 = bf16[8,32,128]{2,1,0:T(8,128)(2,1)S(1)} custom-call(bf16[256,96]{1,0:T(8,128)(2,1)S(1)} %get-tuple-element.25.grad_pre, bf16[2,96,96]{2,1,0:T(8,128)(2,1)S(1)} %get-tuple-element.26.first, bf16[256,256]{1,0:T(8,128)(2,1)S(1)} %get-tuple-element.27.lat_t), custom_call_target="tpu_custom_call" | custom-call | flops 37748736 | bytes 262144 | tf_op jit(solution)/shard_map/grad_lat/pallas_call | solution.py:365
  22.3 0.5 %collective-permute-done.1 = bf16[2,80,128]{2,1,0:T(8,128)(2,1)S(1)} collective-permute-done((bf16[2,80,128]{2,1,0:T(8,128)(2,1)S(1)}, bf16[2,80,128]{2,1,0:T(8,128)(2,1)S(1)}, u32[]{:S(2)}, u32[]{:S(2)}) %collective-permute-start.1) | collective-permute-done | bytes 40992 | tf_op jit(solution)/shard_map/ppermute | solution.py:386
  22.8 9.0 %all_to_all.11.pieces = bf16[8,112,128]{2,1,0:T(8,128)(2,1)S(1)} all-to-all(bf16[8,112,128]{2,1,0:T(8,128)(2,1)S(1)} %pad_maximum_fusion), channel_id=1, replica_groups=mesh['dp'=4,'space'=8] {'space'}, dimensions={0} | all-to-all | bytes 458752 | tf_op jit(solution)/shard_map/all_to_all | solution.py:389
  31.8 0.1 collective-permute-start.2
  31.9 1.4 %inverse_lon.1 = bf16[180,2,768]{2,1,0:T(2,128)(2,1)} custom-call(bf16[360,32]{1,0:T(8,128)(2,1)S(1)} %get-tuple-element.19.table, bf16[8,112,128]{2,1,0:T(8,128)(2,1)S(1)} %all_to_all.11.pieces), custom_call_target="tpu_custom_call" | custom-call | flops 17694720 | bytes 2211840 | tf_op jit(solution)/shard_map/inverse_lon/pallas_call | solution.py:399
  33.4 0.0 collective-permute-done.2.others
  33.4 0.9 %gathered.1 = (f32[2,192,96]{2,1,0:T(8,128)}, f32[2,192,96]{2,1,0:T(8,128)}, f32[2,192]{1,0:T(2,128)}, f32[2,192]{1,0:T(2,128)}) custom-call(bf16[8,112,128]{2,1,0:T(8,128)(2,1)S(1)} %all_to_all.11.pieces, bf16[8,80,128]{2,1,0:T(8,128)(2,1)S(1)} %collective-permute-done.2.others), custom_call_target="tpu_custom_call" | custom-call | tf_op jit(solution)/shard_map/gathered/pallas_call | solution.py:410
  (5 shorter events, 0.1 us)
Async XLA Ops:
  15.3 0.7 %collective-permute-start = (bf16[2,2,80,128]{3,2,1,0:T(8,128)(2,1)S(1)}, bf16[2,2,80,128]{3,2,1,0:T(8,128)(2,1)S(1)}, u32[]{:S(2)}, u32[]{:S(2)}) collective-permute-start(bf16[2,2,80,128]{3,2,1,0:T(8,128)(2,1)S(1)} %get-tuple-element.28), channel_id=1, source_target_pairs={{0,0},{1,9},{2,2},{3,11},{4,20},{5,29},{6,22},{7,31},{8,16},{9,25}... | collective-permute-start | bytes 245768 | tf_op jit(solution)/shard_map/ppermute | solution.py:377
  15.9 6.8 %collective-permute-start.1 = (bf16[2,80,128]{2,1,0:T(8,128)(2,1)S(1)}, bf16[2,80,128]{2,1,0:T(8,128)(2,1)S(1)}, u32[]{:S(2)}, u32[]{:S(2)}) collective-permute-start(bf16[2,80,128]{2,1,0:T(8,128)(2,1)S(1)} %slice_bitcast_fusion), channel_id=1, source_target_pairs={{0,1},{1,0},{2,3},{3,2},{4,5},{5,4},{6,7},{7,6},{8,9},{9,8},{10,11... | collective-permute-start | bytes 122888 | tf_op jit(solution)/shard_map/ppermute | solution.py:386
  31.8 1.5 %collective-permute-start.2 = (bf16[8,80,128]{2,1,0:T(8,128)(2,1)S(1)}, bf16[8,80,128]{2,1,0:T(8,128)(2,1)S(1)}, u32[]{:S(2)}, u32[]{:S(2)}) collective-permute-start(bf16[8,80,128]{2,1,0:T(8,128)(2,1)S(1)} %slice.14), channel_id=1, source_target_pairs={{0,1},{1,0},{2,3},{3,2},{4,5},{5,4},{6,7},{7,6},{8,9},{9,8},{10,11... | collective-permute-start | bytes 491528 | tf_op jit(solution)/shard_map/ppermute | solution.py:396
where the time goes:
time: 34.5 us; the launch traced here: 34.2 us
  blocking collectives  20.2 us (59%)
  starting transfers between devices  6.66 us (19%)
  Pallas kernels  6.09 us (18%)
  between operations  0.71 us (2%)
  waiting for transfers between devices  0.49 us (1%)
    all_to_all x1, blocking collectives, by_blocks(): pieces = lax.all_to_all(sent, 'space', 0, 0, tiled=True)  11.2 us
    all_to_all x1, blocking collectives, by_blocks(): lax.all_to_all(jnp.concatenate([grad_lat, share.reshape(parts, term_rows,...  9.01 us
    ppermute x1, starting transfers between devices, by_blocks(): lax.ppermute(arrived[1], 'space', [(c, c ^ 1) for c in range(parts)])  5.92 us
    pallas_call x1, Pallas kernels, by_blocks(): pl.pallas_call(forward_lon_kernel, out_shape=(pltpu.VMEM((parts, height,...  2.58 us
    pallas_call x1, Pallas kernels, by_blocks(): pl.pallas_call(functools.partial(inverse_lon_kernel, ortho_scale=ortho_sc...  1.44 us
    pallas_call x1, Pallas kernels, by_blocks(): pl.pallas_call(functools.partial(gathered_kernel, grad_norm=grad_norm), o...  0.87 us
    pallas_call x1, Pallas kernels, by_blocks(): pl.pallas_call(functools.partial(spectral_kernel, ortho_scale=ortho_scale...  0.82 us
  transfers between devices with their start and end apart: 3, of which 1 were waited for; matrix products, arithmetic and copies ran while one was open for 0% of the time, Pallas kernels for 5%

commit v1 on v0

--- a/solution.py
+++ b/solution.py
@@ -18,6 +18,7 @@
 F32 = jnp.float32
 LANES = 128
 THIRD = LANES - BS
+LON_CUT = 96
 VMEM_LIMIT = 32 * 1024 * 1024
 
 
@@ -177,13 +178,24 @@
 
 def block_adjoint(operand, matrix):
     half = operand.shape[0] // 2
-    real = dot(operand, matrix[0], 1, 0)
-    imag = dot(operand, matrix[1], 1, 0)
+    both = dot(operand, matrix, 1, 0)
+    real, imag = both[:, :LANES], both[:, LANES:]
     return jnp.concatenate([real[:half] + imag[half:], real[half:] - imag[:half]], axis=0)
 
 
 def spectral_kernel(
-    pieces, first_wide, second_wide, bias_wide, lat, terms, grad_pre_out, first_out, *, ortho_scale, rows, kept
+    pieces,
+    first_wide,
+    second_wide,
+    bias_wide,
+    lat,
+    terms,
+    grad_pre_out,
+    first_out,
+    *,
+    ortho_scale,
+    rows,
+    kept,
 ):
     device = lax.axis_index("space")
     _, offset = window_of(block_of(lax.axis_index("dp"), device))
@@ -191,86 +203,108 @@
     per = rows * 2 * kept
     half = parts * per // 2
     modes = half // kept
-    chosen = lax.broadcasted_iota(jnp.int32, (2 * LANES, BS), 0) == (
-        lax.broadcasted_iota(jnp.int32, (2 * LANES, BS), 1) + offset
+    spare = jnp.zeros((LANES - BS, LANES), F32)
+    place = lax.broadcasted_iota(jnp.int32, (2 * LANES, LANES), 1)
+    chosen = (lax.broadcasted_iota(jnp.int32, (2 * LANES, LANES), 0) == place + offset) & (
+        place < BS
     )
     chosen = jnp.where(chosen, 1.0, 0.0).astype(BF)
-    first = [dot(first_wide[p], chosen, 1, 0).astype(BF) for p in range(2)]
-    second = [dot(second_wide[p], chosen, 1, 0).astype(BF) for p in range(2)]
-    bias = pltpu.roll(bias_wide[...], (2 * LANES - offset) % (2 * LANES), 1)
-    opened = [unfold(pieces[i]) for i in range(parts)]
-
-    def spectrum(t):
-        stacked = jnp.concatenate([piece[t * per : (t + 1) * per] for piece in opened], axis=0)
-        return (dot(lat[...], stacked, 1, 0) * ortho_scale).astype(BF)
-
-    def mask(k):
-        start = 2 * per + k * 2 * modes
+
+    def matrices(wide):
+        found = dot(wide[...].reshape(2 * BS, 2 * LANES), chosen, 1, 0)
+        return [jnp.concatenate([found[p * BS : (p + 1) * BS], spare], axis=0) for p in range(2)]
+
+    first, second = matrices(first_wide), matrices(second_wide)
+    across = jnp.concatenate(first, axis=0).astype(BF)
+    first_out[...] = jnp.concatenate(first, axis=1).astype(BF)
+    second = jnp.concatenate(second, axis=1).astype(BF)
+    bias = pltpu.roll(bias_wide[...], (2 * LANES - offset) % (2 * LANES), 1)[:, :LANES]
+    bias = jnp.where(lax.broadcasted_iota(jnp.int32, bias.shape, 1) < BS, bias, 0.0)
+
+    def mode_rows(found):
         return jnp.concatenate(
-            [
-                opened[j][start + p * modes : start + (p + 1) * modes]
-                for p in range(2)
-                for j in range(kept)
-            ],
-            axis=0,
+            [found[j][p * modes : (p + 1) * modes] for p in range(2) for j in range(kept)], axis=0
         ).astype(F32)
 
-    spec_act = spectrum(0)
-    spec_cot = spectrum(1)
-    passed = mask(0) > 0.0
-    weight = mask(1)
+    group = pieces.shape[1] // 3
+    passed = mode_rows([pieces[j, 2 * per :, :] for j in range(kept)]) > 0.0
+    weight = mode_rows(
+        [
+            jnp.concatenate(
+                [pieces[j, g * group : (g + 1) * group, BS:] for g in range(3)]
+                + [jnp.zeros((group, THIRD), BF)],
+                axis=1,
+            )
+            for j in range(kept)
+        ]
+    )
+
+    stacked = jnp.concatenate(
+        [
+            jnp.concatenate([pieces[i, t * per : (t + 1) * per, :] for i in range(parts)], axis=0)
+            for t in range(2)
+        ],
+        axis=1,
+    )
+    spectra = (dot(lat[...], stacked, 1, 0) * ortho_scale).astype(BF)
+    spec_act, spec_cot = spectra[:, :LANES], spectra[:, LANES:]
     grad_out = jnp.where(weight > 0.0, weight * spec_cot.astype(F32), 0.0).astype(BF)
-
-    by_real = dot(spec_act, first[0], 1, 1)
-    by_imag = dot(spec_act, first[1], 1, 1)
+    grad_pre = jnp.where(passed, block_adjoint(grad_out, second), 0.0).astype(BF)
+    grad_pre_out[...] = grad_pre
+
+    both = dot(spec_act, across, 1, 1)
+    by_real, by_imag = both[:, :LANES], both[:, LANES:]
     pre = jnp.concatenate(
         [
-            by_real[:half] - by_imag[half:] + bias[0:1, :BS],
-            by_imag[:half] + by_real[half:] + bias[1:2, :BS],
+            by_real[:half] - by_imag[half:] + bias[0:1],
+            by_imag[:half] + by_real[half:] + bias[1:2],
         ],
         axis=0,
     )
     hidden = jnp.where(passed, pre, 0.0).astype(BF)
-
-    grad_pre = jnp.where(passed, block_adjoint(grad_out, second), 0.0).astype(BF)
-    grad_pre_out[...] = grad_pre
-    for p in range(2):
-        first_out[p] = first[p]
-
-    def turned(array):
-        return jnp.concatenate([array[half:], -array[:half]], axis=0)
 
     at = 3 * BS // 4
     blank = jnp.zeros((terms.shape[2] - at - 1, LANES), F32)
     for a, (left, right) in enumerate(((spec_act, grad_pre), (hidden, grad_out))):
         slot = (a + device) % 2
         wide = right.astype(F32)
-        for p, other in enumerate((right, turned(right))):
+        turned = jnp.concatenate([right[half:], -right[:half]], axis=0)
+        products = dot(left, jnp.concatenate([right, turned], axis=1), 0, 0)
+        for p in range(2):
             summed = jnp.sum(wide[p * half : (p + 1) * half], axis=0, keepdims=True)
-            summed = jnp.concatenate([summed, jnp.zeros((1, THIRD), F32)], axis=1)
             terms[slot, p] = jnp.concatenate(
-                [fold(dot(left, other, 0, 0)), summed, blank], axis=0
+                [fold(products[:BS, p * LANES : p * LANES + BS]), summed, blank], axis=0
             ).astype(BF)
 
 
 def grad_lat_kernel(grad_pre, first, lat_t, grad_lat):
-    grad_spec = block_adjoint(grad_pre[...], first).astype(BF)
+    grad_spec = block_adjoint(grad_pre[...], first[...]).astype(BF)
     lines = dot(lat_t[...], grad_spec, 1, 0)
-    lines = jnp.concatenate([lines, jnp.zeros((lines.shape[0], THIRD), F32)], axis=1).astype(BF)
-    grad_lat[...] = lines.reshape(grad_lat.shape)
-
-
-def inverse_lon_kernel(table, pieces, field, *, ortho_scale):
+    per = lines.shape[0] // grad_lat.shape[0]
+    for i in range(grad_lat.shape[0]):
+        grad_lat[i] = fold(lines[i * per : (i + 1) * per, :BS]).astype(BF)
+
+
+def inverse_lon_kernel(table, pieces, field_hbm, field, sems, *, ortho_scale):
     rows = field.shape[1]
     per = table.shape[1]
     group = lax.axis_index("dp")
     lines = jnp.concatenate(
-        [pieces[owner_of(group, b), 0:per, 0:BS] for b in range(BLOCKS)], axis=1
-    )
-    wide = (dot(table[...], lines, 1, 0) * ortho_scale).astype(BF)
-    for k in range(C // LANES):
-        lanes = slice(k * LANES, (k + 1) * LANES)
-        field[:, :, lanes] = wide[:, lanes].reshape(LON, rows, LANES)
+        [unfold(pieces[owner_of(group, b), 0 : 3 * per // 4, :]) for b in range(BLOCKS)], axis=1
+    )
+    copies = []
+    for i, (start, stop) in enumerate(((0, LON_CUT), (LON_CUT, LON))):
+        wide = (dot(table[start * rows : stop * rows], lines, 1, 0) * ortho_scale).astype(BF)
+        for k in range(C // LANES):
+            lanes = slice(k * LANES, (k + 1) * LANES)
+            field[start:stop, :, lanes] = wide[:, lanes].reshape(stop - start, rows, LANES)
+        copy = pltpu.make_async_copy(
+            field.at[start:stop], field_hbm.at[start:stop], sems.at[i]
+        )
+        copy.start()
+        copies.append(copy)
+    for copy in copies:
+        copy.wait()
 
 
 def gathered_kernel(pieces, others, first, second, bias_first, bias_second, *, grad_norm):
@@ -354,8 +388,8 @@
         functools.partial(spectral_kernel, ortho_scale=ortho_scale, rows=rows, kept=kept),
         out_shape=(
             jax.ShapeDtypeStruct((2, 2, term_rows, LANES), BF),
-            pltpu.VMEM((lat.shape[0], BS), BF),
-            pltpu.VMEM((2, BS, BS), BF),
+            pltpu.VMEM((lat.shape[0], LANES), BF),
+            pltpu.VMEM((LANES, 2 * LANES), BF),
         ),
         in_specs=[whole()] * 5,
         out_specs=(whole(),) * 3,
@@ -364,7 +398,7 @@
     )(pieces, *fetched)
     grad_lat = pl.pallas_call(
         grad_lat_kernel,
-        out_shape=jax.ShapeDtypeStruct((parts, per, LANES), BF),
+        out_shape=jax.ShapeDtypeStruct((parts, 3 * per // 4, LANES), BF),
         in_specs=[whole()] * 3,
         out_specs=whole(),
         compiler_params=params,
@@ -393,14 +427,18 @@
         0,
         tiled=True,
     )
-    others = lax.ppermute(returned[:, per:, :], "space", [(c, c ^ 1) for c in range(parts)])
+    others = lax.ppermute(returned[:, 3 * per // 4 :, :], "space", [(c, c ^ 1) for c in range(parts)])
 
     keep_rows = C // groups
     field = pl.pallas_call(
         functools.partial(inverse_lon_kernel, ortho_scale=ortho_scale),
         out_shape=jax.ShapeDtypeStruct((LON, rows, C), BF),
         in_specs=[whole(), whole()],
-        out_specs=whole(),
+        out_specs=whole(pl.ANY),
+        scratch_shapes=[
+            pltpu.VMEM((LON, rows, C), BF),
+            pltpu.SemaphoreType.DMA((2,)),
+        ],
         compiler_params=params,
         cost_estimate=pl.CostEstimate(
             flops=2 * per * LON * rows * C, bytes_accessed=8 * LON * rows * C, transcendentals=0

time: 34.5 us -> 34.3 us (level)
  transfers between devices with their start and end apart: 3 -> 3, of which waited for: 1 -> 1; matrix products, arithmetic and copies ran while one was open for 0% -> 0% of each run, Pallas kernels for 5% -> 6%
where the time goes in v1:
time: 34.3 us; the launch traced here: 34.1 us
  blocking collectives  20 us (58%)
  starting transfers between devices  6.66 us (19%)
  Pallas kernels  6.21 us (18%)
  between operations  0.72 us (2%)
  waiting for transfers between devices  0.36 us (1%)
    all_to_all x1, blocking collectives, by_blocks(): pieces = lax.all_to_all(sent, 'space', 0, 0, tiled=True)  11.2 us
    all_to_all x1, blocking collectives, by_blocks(): lax.all_to_all(jnp.concatenate([grad_lat, share.reshape(parts, term_rows,...  8.84 us
    ppermute x1, starting transfers between devices, by_blocks(): lax.ppermute(arrived[1], 'space', [(c, c ^ 1) for c in range(parts)])  5.92 us
    pallas_call x1, Pallas kernels, by_blocks(): pl.pallas_call(forward_lon_kernel, out_shape=(pltpu.VMEM((parts, height,...  2.58 us
    pallas_call x1, Pallas kernels, by_blocks(): pl.pallas_call(functools.partial(inverse_lon_kernel, ortho_scale=ortho_sc...  1.45 us
    pallas_call x1, Pallas kernels, by_blocks(): pl.pallas_call(functools.partial(gathered_kernel, grad_norm=grad_norm), o...  0.87 us
    pallas_call x1, Pallas kernels, by_blocks(): pl.pallas_call(functools.partial(spectral_kernel, ortho_scale=ortho_scale...  0.79 us
  transfers between devices with their start and end apart: 3, of which 1 were waited for; matrix products, arithmetic and copies ran while one was open for 0% of the time, Pallas kernels for 6%

profile of v1, /device:TPU:0, one launch (start us, length us, event | category | flops | bytes accessed | tf_op | source)
XLA Modules:
  0.0 34.1 jit_solution(8616845334620887632)
XLA Ops:
  0.6 2.6 %forward_lon.1 = (bf16[8,96,128]{2,1,0:T(8,128)(2,1)S(1)}, bf16[360,32]{1,0:T(8,128)(2,1)S(1)}, bf16[2,96,256]{2,1,0:T(8,128)(2,1)S(1)}, bf16[2,96,256]{2,1,0:T(...) custom-call(s32[8]{0:T(128)} %keep_hbm.1, ...), custom_call_target="tpu_custom_call" | custom-call | tf_op jit(solution)/shard_map/forward_lon/pallas_call | solution.py:346
  3.2 11.2 %all_to_all.10.pieces = bf16[8,96,128]{2,1,0:T(8,128)(2,1)S(1)} all-to-all(bf16[8,96,128]{2,1,0:T(8,128)(2,1)S(1)} %get-tuple-element.20), channel_id=1, replica_groups=mesh['dp'=4,'space'=8] {'space'}, dimensions={0} | all-to-all | bytes 393216 | tf_op jit(solution)/shard_map/all_to_all | solution.py:384
  14.4 0.8 %spectral.1 = (bf16[2,2,80,128]{3,2,1,0:T(8,128)(2,1)S(1)}, bf16[256,128]{1,0:T(8,128)(2,1)S(1)}, bf16[128,256]{1,0:T(8,128)(2,1)S(1)}) custom-call(bf16[8,96,128]{2,1,0:T(8,128)(2,1)S(1)} %all_to_all.10.pieces, bf16[2,96,256]{2,1,0:T(8,128)(2,1)S(1)} %get-tuple-element.21.first_wide, bf16[2,96,256]{2,1,0:T(8,128)(2,1)S(1)} %get-tuple-element.22.second_wide, ...), custom_call_target="tpu_custom_call" | custom-call | tf_op jit(solution)/shard_map/spectral/pallas_call | solution.py:387
  15.2 0.7 %collective-permute-start = (bf16[2,2,80,128]{3,2,1,0:T(8,128)(2,1)S(1)}, bf16[2,2,80,128]{3,2,1,0:T(8,128)(2,1)S(1)}, u32[]{:S(2)}, u32[]{:S(2)}) collective-permute-start(bf16[2,2,80,128]{3,2,1,0:T(8,128)(2,1)S(1)} %get-tuple-element.28), channel_id=1, source_target_pairs={{0,0},{1,9},{2,2},{3,11},{4,20},{5,29},{6,22},{7,31},{8,16},{9,25}... | collective-permute-start | bytes 245768 | tf_op jit(solution)/shard_map/ppermute | solution.py:411
  15.9 0.0 collective-permute-done
  15.9 5.9 %collective-permute-start.1 = (bf16[2,80,128]{2,1,0:T(8,128)(2,1)S(1)}, bf16[2,80,128]{2,1,0:T(8,128)(2,1)S(1)}, u32[]{:S(2)}, u32[]{:S(2)}) collective-permute-start(bf16[2,80,128]{2,1,0:T(8,128)(2,1)S(1)} %slice_bitcast_fusion), channel_id=1, source_target_pairs={{0,1},{1,0},{2,3},{3,2},{4,5},{5,4},{6,7},{7,6},{8,9},{9,8},{10,11... | collective-permute-start | bytes 122888 | tf_op jit(solution)/shard_map/ppermute | solution.py:420
  21.8 0.5 %grad_lat.1 = bf16[8,24,128]{2,1,0:T(8,128)(2,1)S(1)} custom-call(bf16[256,128]{1,0:T(8,128)(2,1)S(1)} %get-tuple-element.25.grad_pre, bf16[128,256]{1,0:T(8,128)(2,1)S(1)} %get-tuple-element.26.first, bf16[256,256]{1,0:T(8,128)(2,1)S(1)} %get-tuple-element.27.lat_t), custom_call_target="tpu_custom_call" | custom-call | flops 37748736 | bytes 262144 | tf_op jit(solution)/shard_map/grad_lat/pallas_call | solution.py:399
  22.4 0.4 %collective-permute-done.1 = bf16[2,80,128]{2,1,0:T(8,128)(2,1)S(1)} collective-permute-done((bf16[2,80,128]{2,1,0:T(8,128)(2,1)S(1)}, bf16[2,80,128]{2,1,0:T(8,128)(2,1)S(1)}, u32[]{:S(2)}, u32[]{:S(2)}) %collective-permute-start.1) | collective-permute-done | bytes 40992 | tf_op jit(solution)/shard_map/ppermute | solution.py:420
  22.8 8.8 %all_to_all.11.pieces = bf16[8,104,128]{2,1,0:T(8,128)(2,1)S(1)} all-to-all(bf16[8,104,128]{2,1,0:T(8,128)(2,1)S(1)} %pad_maximum_fusion), channel_id=1, replica_groups=mesh['dp'=4,'space'=8] {'space'}, dimensions={0} | all-to-all | bytes 425984 | tf_op jit(solution)/shard_map/all_to_all | solution.py:423
  31.6 0.1 collective-permute-start.2
  31.7 1.5 %inverse_lon.1 = bf16[180,2,768]{2,1,0:T(2,128)(2,1)} custom-call(bf16[360,32]{1,0:T(8,128)(2,1)S(1)} %get-tuple-element.19.table, bf16[8,104,128]{2,1,0:T(8,128)(2,1)S(1)} %all_to_all.11.pieces), custom_call_target="tpu_custom_call" | custom-call | flops 17694720 | bytes 2211840 | tf_op jit(solution)/shard_map/inverse_lon/pallas_call | solution.py:433
  33.2 0.0 collective-permute-done.2.others
  33.2 0.9 %gathered.1 = (f32[2,192,96]{2,1,0:T(8,128)}, f32[2,192,96]{2,1,0:T(8,128)}, f32[2,192]{1,0:T(2,128)}, f32[2,192]{1,0:T(2,128)}) custom-call(bf16[8,104,128]{2,1,0:T(8,128)(2,1)S(1)} %all_to_all.11.pieces, bf16[8,80,128]{2,1,0:T(8,128)(2,1)S(1)} %collective-permute-done.2.others), custom_call_target="tpu_custom_call" | custom-call | tf_op jit(solution)/shard_map/gathered/pallas_call | solution.py:448
  (5 shorter events, 0.1 us)
Async XLA Ops:
  15.2 0.7 %collective-permute-start = (bf16[2,2,80,128]{3,2,1,0:T(8,128)(2,1)S(1)}, bf16[2,2,80,128]{3,2,1,0:T(8,128)(2,1)S(1)}, u32[]{:S(2)}, u32[]{:S(2)}) collective-permute-start(bf16[2,2,80,128]{3,2,1,0:T(8,128)(2,1)S(1)} %get-tuple-element.28), channel_id=1, source_target_pairs={{0,0},{1,9},{2,2},{3,11},{4,20},{5,29},{6,22},{7,31},{8,16},{9,25}... | collective-permute-start | bytes 245768 | tf_op jit(solution)/shard_map/ppermute | solution.py:411
  15.9 6.8 %collective-permute-start.1 = (bf16[2,80,128]{2,1,0:T(8,128)(2,1)S(1)}, bf16[2,80,128]{2,1,0:T(8,128)(2,1)S(1)}, u32[]{:S(2)}, u32[]{:S(2)}) collective-permute-start(bf16[2,80,128]{2,1,0:T(8,128)(2,1)S(1)} %slice_bitcast_fusion), channel_id=1, source_target_pairs={{0,1},{1,0},{2,3},{3,2},{4,5},{5,4},{6,7},{7,6},{8,9},{9,8},{10,11... | collective-permute-start | bytes 122888 | tf_op jit(solution)/shard_map/ppermute | solution.py:420
  31.6 1.5 %collective-permute-start.2 = (bf16[8,80,128]{2,1,0:T(8,128)(2,1)S(1)}, bf16[8,80,128]{2,1,0:T(8,128)(2,1)S(1)}, u32[]{:S(2)}, u32[]{:S(2)}) collective-permute-start(bf16[8,80,128]{2,1,0:T(8,128)(2,1)S(1)} %slice.14), channel_id=1, source_target_pairs={{0,1},{1,0},{2,3},{3,2},{4,5},{5,4},{6,7},{7,6},{8,9},{9,8},{10,11... | collective-permute-start | bytes 491528 | tf_op jit(solution)/shard_map/ppermute | solution.py:430

commit v2 on v1

--- a/solution.py
+++ b/solution.py
@@ -91,29 +91,20 @@
     keep_copy.start()
     mask_copies, field_copies = [], []
     for t, source in enumerate((relu_hbm, shrink_hbm)):
-        for p in range(2):
-            for k in range(tiles):
-                copy = pltpu.make_async_copy(
-                    source.at[:, p, :, columns[k]],
-                    masks.at[t, p, k],
-                    sems.at[1 + (2 * t + p) * tiles + k],
-                )
-                copy.start()
-                mask_copies.append(copy)
+        copy = pltpu.make_async_copy(source, masks.at[t], sems.at[1 + t])
+        copy.start()
+        mask_copies.append(copy)
     for t, source in enumerate((act_hbm, cot_hbm)):
-        for k in range(tiles):
-            copy = pltpu.make_async_copy(
-                source.at[:, :, columns[k]], field.at[t, k], sems.at[1 + (4 + t) * tiles + k]
-            )
-            copy.start()
-            field_copies.append(copy)
+        copy = pltpu.make_async_copy(source, field.at[t], sems.at[3 + t])
+        copy.start()
+        field_copies.append(copy)
     sources = [
         source.at[(slice(None),) * (len(source.shape) - 1) + (pl.ds(start, 2 * LANES),)]
         for source in weights_hbm
     ] + list(matrices_hbm)
     other_copies = []
     for i, (source, target) in enumerate(zip(sources, fetched)):
-        copy = pltpu.make_async_copy(source, target, sems.at[1 + 6 * tiles + i])
+        copy = pltpu.make_async_copy(source, target, sems.at[5 + i])
         copy.start()
         other_copies.append(copy)
 
@@ -138,17 +129,7 @@
 
     def gate(t, value):
         return jnp.concatenate(
-            [
-                jnp.concatenate(
-                    [
-                        jnp.where(masks.at[t, p, k].reshape(modes, LANES)[...] > 0, value, 0.0)
-                        for k in range(tiles)
-                    ],
-                    axis=1,
-                )
-                for p in range(2)
-            ],
-            axis=0,
+            [jnp.where(masks[t, :, p, 0, :] > 0, value, 0.0) for p in range(2)], axis=0
         ).astype(BF)
 
     passed = gate(0, 1.0)
@@ -161,11 +142,10 @@
         out[owners[b], :, BS:] = jnp.concatenate(beside, axis=0)
 
     for t in range(2):
-        for copy in field_copies[t * tiles : (t + 1) * tiles]:
-            copy.wait()
+        field_copies[t].wait()
         wide = jnp.concatenate(
             [
-                field[t, k].reshape(LON * rows, LANES) for k in range(tiles)
+                field[t, :, :, columns[k]].reshape(LON * rows, LANES) for k in range(tiles)
             ],
             axis=1,
         )
@@ -357,10 +337,10 @@
         in_specs=[whole(pl.ANY)] * 10,
         out_specs=(whole(),) * 7,
         scratch_shapes=[
-            pltpu.VMEM((2, tiles, LON, rows, LANES), BF),
-            pltpu.VMEM((2, 2, tiles, lat_len, 1, LANES), jnp.int32),
+            pltpu.VMEM((2, LON, rows, C), BF),
+            pltpu.VMEM((2, lat_len, 2, 1, C), jnp.int32),
             pltpu.SMEM((kept,), jnp.int32),
-            pltpu.SemaphoreType.DMA((6 + 6 * tiles,)),
+            pltpu.SemaphoreType.DMA((10,)),
         ],
         compiler_params=params,
         name="forward_lon",

time: 34.3 us -> 33.9 us (0.988)
  Pallas kernels: 6.21 us -> 5.76 us
    pallas_call x1, Pallas kernels: 2.58 us -> 2.13 us  [by_blocks(): pl.pallas_call(forward_lon_kernel, out_shape=(pltpu.VMEM((parts, height,...]
where the time goes in v2:
time: 33.9 us; the launch traced here: 33.6 us
  blocking collectives  20 us (59%)
  starting transfers between devices  6.66 us (20%)
  Pallas kernels  5.76 us (17%)
  between operations  0.72 us (2%)
  waiting for transfers between devices  0.36 us (1%)
    all_to_all x1, blocking collectives, by_blocks(): pieces = lax.all_to_all(sent, 'space', 0, 0, tiled=True)  11.2 us
    all_to_all x1, blocking collectives, by_blocks(): lax.all_to_all(jnp.concatenate([grad_lat, share.reshape(parts, term_rows,...  8.84 us
    ppermute x1, starting transfers between devices, by_blocks(): lax.ppermute(arrived[1], 'space', [(c, c ^ 1) for c in range(parts)])  5.92 us
    pallas_call x1, Pallas kernels, by_blocks(): pl.pallas_call(forward_lon_kernel, out_shape=(pltpu.VMEM((parts, height,...  2.13 us
    pallas_call x1, Pallas kernels, by_blocks(): pl.pallas_call(functools.partial(inverse_lon_kernel, ortho_scale=ortho_sc...  1.45 us
    pallas_call x1, Pallas kernels, by_blocks(): pl.pallas_call(functools.partial(gathered_kernel, grad_norm=grad_norm), o...  0.87 us
    pallas_call x1, Pallas kernels, by_blocks(): pl.pallas_call(functools.partial(spectral_kernel, ortho_scale=ortho_scale...  0.79 us
  transfers between devices with their start and end apart: 3, of which 1 were waited for; matrix products, arithmetic and copies ran while one was open for 0% of the time, Pallas kernels for 6%

profile of v2, /device:TPU:0, one launch (start us, length us, event | category | flops | bytes accessed | tf_op | source)
XLA Modules:
  0.0 33.6 jit_solution(9434654714475737457)
XLA Ops:
  0.6 2.1 %forward_lon.1 = (bf16[8,96,128]{2,1,0:T(8,128)(2,1)S(1)}, bf16[360,32]{1,0:T(8,128)(2,1)S(1)}, bf16[2,96,256]{2,1,0:T(8,128)(2,1)S(1)}, bf16[2,96,256]{2,1,0:T(...) custom-call(s32[8]{0:T(128)} %keep_hbm.1, ...), custom_call_target="tpu_custom_call" | custom-call | tf_op jit(solution)/shard_map/forward_lon/pallas_call | solution.py:326
  2.8 11.2 %all_to_all.10.pieces = bf16[8,96,128]{2,1,0:T(8,128)(2,1)S(1)} all-to-all(bf16[8,96,128]{2,1,0:T(8,128)(2,1)S(1)} %get-tuple-element.20), channel_id=1, replica_groups=mesh['dp'=4,'space'=8] {'space'}, dimensions={0} | all-to-all | bytes 393216 | tf_op jit(solution)/shard_map/all_to_all | solution.py:364
  14.0 0.8 %spectral.1 = (bf16[2,2,80,128]{3,2,1,0:T(8,128)(2,1)S(1)}, bf16[256,128]{1,0:T(8,128)(2,1)S(1)}, bf16[128,256]{1,0:T(8,128)(2,1)S(1)}) custom-call(bf16[8,96,128]{2,1,0:T(8,128)(2,1)S(1)} %all_to_all.10.pieces, bf16[2,96,256]{2,1,0:T(8,128)(2,1)S(1)} %get-tuple-element.21.first_wide, bf16[2,96,256]{2,1,0:T(8,128)(2,1)S(1)} %get-tuple-element.22.second_wide, ...), custom_call_target="tpu_custom_call" | custom-call | tf_op jit(solution)/shard_map/spectral/pallas_call | solution.py:367
  14.8 0.7 %collective-permute-start = (bf16[2,2,80,128]{3,2,1,0:T(8,128)(2,1)S(1)}, bf16[2,2,80,128]{3,2,1,0:T(8,128)(2,1)S(1)}, u32[]{:S(2)}, u32[]{:S(2)}) collective-permute-start(bf16[2,2,80,128]{3,2,1,0:T(8,128)(2,1)S(1)} %get-tuple-element.28), channel_id=1, source_target_pairs={{0,0},{1,9},{2,2},{3,11},{4,20},{5,29},{6,22},{7,31},{8,16},{9,25}... | collective-permute-start | bytes 245768 | tf_op jit(solution)/shard_map/ppermute | solution.py:391
  15.4 0.0 collective-permute-done
  15.5 5.9 %collective-permute-start.1 = (bf16[2,80,128]{2,1,0:T(8,128)(2,1)S(1)}, bf16[2,80,128]{2,1,0:T(8,128)(2,1)S(1)}, u32[]{:S(2)}, u32[]{:S(2)}) collective-permute-start(bf16[2,80,128]{2,1,0:T(8,128)(2,1)S(1)} %slice_bitcast_fusion), channel_id=1, source_target_pairs={{0,1},{1,0},{2,3},{3,2},{4,5},{5,4},{6,7},{7,6},{8,9},{9,8},{10,11... | collective-permute-start | bytes 122888 | tf_op jit(solution)/shard_map/ppermute | solution.py:400
  21.4 0.5 %grad_lat.1 = bf16[8,24,128]{2,1,0:T(8,128)(2,1)S(1)} custom-call(bf16[256,128]{1,0:T(8,128)(2,1)S(1)} %get-tuple-element.25.grad_pre, bf16[128,256]{1,0:T(8,128)(2,1)S(1)} %get-tuple-element.26.first, bf16[256,256]{1,0:T(8,128)(2,1)S(1)} %get-tuple-element.27.lat_t), custom_call_target="tpu_custom_call" | custom-call | flops 37748736 | bytes 262144 | tf_op jit(solution)/shard_map/grad_lat/pallas_call | solution.py:379
  21.9 0.4 %collective-permute-done.1 = bf16[2,80,128]{2,1,0:T(8,128)(2,1)S(1)} collective-permute-done((bf16[2,80,128]{2,1,0:T(8,128)(2,1)S(1)}, bf16[2,80,128]{2,1,0:T(8,128)(2,1)S(1)}, u32[]{:S(2)}, u32[]{:S(2)}) %collective-permute-start.1) | collective-permute-done | bytes 40992 | tf_op jit(solution)/shard_map/ppermute | solution.py:400
  22.3 8.8 %all_to_all.11.pieces = bf16[8,104,128]{2,1,0:T(8,128)(2,1)S(1)} all-to-all(bf16[8,104,128]{2,1,0:T(8,128)(2,1)S(1)} %pad_maximum_fusion), channel_id=1, replica_groups=mesh['dp'=4,'space'=8] {'space'}, dimensions={0} | all-to-all | bytes 425984 | tf_op jit(solution)/shard_map/all_to_all | solution.py:403
  31.2 0.1 collective-permute-start.2
  31.3 1.4 %inverse_lon.1 = bf16[180,2,768]{2,1,0:T(2,128)(2,1)} custom-call(bf16[360,32]{1,0:T(8,128)(2,1)S(1)} %get-tuple-element.19.table, bf16[8,104,128]{2,1,0:T(8,128)(2,1)S(1)} %all_to_all.11.pieces), custom_call_target="tpu_custom_call" | custom-call | flops 17694720 | bytes 2211840 | tf_op jit(solution)/shard_map/inverse_lon/pallas_call | solution.py:413
  32.7 0.0 collective-permute-done.2.others
  32.7 0.9 %gathered.1 = (f32[2,192,96]{2,1,0:T(8,128)}, f32[2,192,96]{2,1,0:T(8,128)}, f32[2,192]{1,0:T(2,128)}, f32[2,192]{1,0:T(2,128)}) custom-call(bf16[8,104,128]{2,1,0:T(8,128)(2,1)S(1)} %all_to_all.11.pieces, bf16[8,80,128]{2,1,0:T(8,128)(2,1)S(1)} %collective-permute-done.2.others), custom_call_target="tpu_custom_call" | custom-call | tf_op jit(solution)/shard_map/gathered/pallas_call | solution.py:428
  (5 shorter events, 0.1 us)
Async XLA Ops:
  14.8 0.7 %collective-permute-start = (bf16[2,2,80,128]{3,2,1,0:T(8,128)(2,1)S(1)}, bf16[2,2,80,128]{3,2,1,0:T(8,128)(2,1)S(1)}, u32[]{:S(2)}, u32[]{:S(2)}) collective-permute-start(bf16[2,2,80,128]{3,2,1,0:T(8,128)(2,1)S(1)} %get-tuple-element.28), channel_id=1, source_target_pairs={{0,0},{1,9},{2,2},{3,11},{4,20},{5,29},{6,22},{7,31},{8,16},{9,25}... | collective-permute-start | bytes 245768 | tf_op jit(solution)/shard_map/ppermute | solution.py:391
  15.5 6.8 %collective-permute-start.1 = (bf16[2,80,128]{2,1,0:T(8,128)(2,1)S(1)}, bf16[2,80,128]{2,1,0:T(8,128)(2,1)S(1)}, u32[]{:S(2)}, u32[]{:S(2)}) collective-permute-start(bf16[2,80,128]{2,1,0:T(8,128)(2,1)S(1)} %slice_bitcast_fusion), channel_id=1, source_target_pairs={{0,1},{1,0},{2,3},{3,2},{4,5},{5,4},{6,7},{7,6},{8,9},{9,8},{10,11... | collective-permute-start | bytes 122888 | tf_op jit(solution)/shard_map/ppermute | solution.py:400
  31.2 1.5 %collective-permute-start.2 = (bf16[8,80,128]{2,1,0:T(8,128)(2,1)S(1)}, bf16[8,80,128]{2,1,0:T(8,128)(2,1)S(1)}, u32[]{:S(2)}, u32[]{:S(2)}) collective-permute-start(bf16[8,80,128]{2,1,0:T(8,128)(2,1)S(1)} %slice.14), channel_id=1, source_target_pairs={{0,1},{1,0},{2,3},{3,2},{4,5},{5,4},{6,7},{7,6},{8,9},{9,8},{10,11... | collective-permute-start | bytes 491528 | tf_op jit(solution)/shard_map/ppermute | solution.py:410

commit v3 on v2

--- a/solution.py
+++ b/solution.py
@@ -90,14 +90,14 @@
     keep_copy = pltpu.make_async_copy(keep_hbm, keep, sems.at[0])
     keep_copy.start()
     mask_copies, field_copies = [], []
+    for t, source in enumerate((act_hbm, cot_hbm)):
+        copy = pltpu.make_async_copy(source, field.at[t], sems.at[3 + t])
+        copy.start()
+        field_copies.append(copy)
     for t, source in enumerate((relu_hbm, shrink_hbm)):
         copy = pltpu.make_async_copy(source, masks.at[t], sems.at[1 + t])
         copy.start()
         mask_copies.append(copy)
-    for t, source in enumerate((act_hbm, cot_hbm)):
-        copy = pltpu.make_async_copy(source, field.at[t], sems.at[3 + t])
-        copy.start()
-        field_copies.append(copy)
     sources = [
         source.at[(slice(None),) * (len(source.shape) - 1) + (pl.ds(start, 2 * LANES),)]
         for source in weights_hbm

time: 33.9 us -> 34.1 us (level)
  no operation moved by 1% of the time
where the time goes in v3:
time: 34.1 us; the launch traced here: 33.9 us
  blocking collectives  20 us (59%)
  starting transfers between devices  6.66 us (20%)
  Pallas kernels  6.03 us (18%)
  between operations  0.72 us (2%)
  waiting for transfers between devices  0.36 us (1%)
    all_to_all x1, blocking collectives, by_blocks(): pieces = lax.all_to_all(sent, 'space', 0, 0, tiled=True)  11.2 us
    all_to_all x1, blocking collectives, by_blocks(): lax.all_to_all(jnp.concatenate([grad_lat, share.reshape(parts, term_rows,...  8.84 us
    ppermute x1, starting transfers between devices, by_blocks(): lax.ppermute(arrived[1], 'space', [(c, c ^ 1) for c in range(parts)])  5.92 us
    pallas_call x1, Pallas kernels, by_blocks(): pl.pallas_call(forward_lon_kernel, out_shape=(pltpu.VMEM((parts, height,...  2.4 us
    pallas_call x1, Pallas kernels, by_blocks(): pl.pallas_call(functools.partial(inverse_lon_kernel, ortho_scale=ortho_sc...  1.45 us
    pallas_call x1, Pallas kernels, by_blocks(): pl.pallas_call(functools.partial(gathered_kernel, grad_norm=grad_norm), o...  0.87 us
    pallas_call x1, Pallas kernels, by_blocks(): pl.pallas_call(functools.partial(spectral_kernel, ortho_scale=ortho_scale...  0.79 us
  transfers between devices with their start and end apart: 3, of which 1 were waited for; matrix products, arithmetic and copies ran while one was open for 0% of the time, Pallas kernels for 6%

profile of v3, /device:TPU:0, one launch (start us, length us, event | category | flops | bytes accessed | tf_op | source)
XLA Modules:
  0.0 33.9 jit_solution(330428054752760907)
XLA Ops:
  0.6 2.4 %forward_lon.1 = (bf16[8,96,128]{2,1,0:T(8,128)(2,1)S(1)}, bf16[360,32]{1,0:T(8,128)(2,1)S(1)}, bf16[2,96,256]{2,1,0:T(8,128)(2,1)S(1)}, bf16[2,96,256]{2,1,0:T(...) custom-call(s32[8]{0:T(128)} %keep_hbm.1, ...), custom_call_target="tpu_custom_call" | custom-call | tf_op jit(solution)/shard_map/forward_lon/pallas_call | solution.py:326
  3.0 11.2 %all_to_all.10.pieces = bf16[8,96,128]{2,1,0:T(8,128)(2,1)S(1)} all-to-all(bf16[8,96,128]{2,1,0:T(8,128)(2,1)S(1)} %get-tuple-element.20), channel_id=1, replica_groups=mesh['dp'=4,'space'=8] {'space'}, dimensions={0} | all-to-all | bytes 393216 | tf_op jit(solution)/shard_map/all_to_all | solution.py:364
  14.2 0.8 %spectral.1 = (bf16[2,2,80,128]{3,2,1,0:T(8,128)(2,1)S(1)}, bf16[256,128]{1,0:T(8,128)(2,1)S(1)}, bf16[128,256]{1,0:T(8,128)(2,1)S(1)}) custom-call(bf16[8,96,128]{2,1,0:T(8,128)(2,1)S(1)} %all_to_all.10.pieces, bf16[2,96,256]{2,1,0:T(8,128)(2,1)S(1)} %get-tuple-element.21.first_wide, bf16[2,96,256]{2,1,0:T(8,128)(2,1)S(1)} %get-tuple-element.22.second_wide, ...), custom_call_target="tpu_custom_call" | custom-call | tf_op jit(solution)/shard_map/spectral/pallas_call | solution.py:367
  15.0 0.7 %collective-permute-start = (bf16[2,2,80,128]{3,2,1,0:T(8,128)(2,1)S(1)}, bf16[2,2,80,128]{3,2,1,0:T(8,128)(2,1)S(1)}, u32[]{:S(2)}, u32[]{:S(2)}) collective-permute-start(bf16[2,2,80,128]{3,2,1,0:T(8,128)(2,1)S(1)} %get-tuple-element.28), channel_id=1, source_target_pairs={{0,0},{1,9},{2,2},{3,11},{4,20},{5,29},{6,22},{7,31},{8,16},{9,25}... | collective-permute-start | bytes 245768 | tf_op jit(solution)/shard_map/ppermute | solution.py:391
  15.7 0.0 collective-permute-done
  15.7 5.9 %collective-permute-start.1 = (bf16[2,80,128]{2,1,0:T(8,128)(2,1)S(1)}, bf16[2,80,128]{2,1,0:T(8,128)(2,1)S(1)}, u32[]{:S(2)}, u32[]{:S(2)}) collective-permute-start(bf16[2,80,128]{2,1,0:T(8,128)(2,1)S(1)} %slice_bitcast_fusion), channel_id=1, source_target_pairs={{0,1},{1,0},{2,3},{3,2},{4,5},{5,4},{6,7},{7,6},{8,9},{9,8},{10,11... | collective-permute-start | bytes 122888 | tf_op jit(solution)/shard_map/ppermute | solution.py:400
  21.7 0.5 %grad_lat.1 = bf16[8,24,128]{2,1,0:T(8,128)(2,1)S(1)} custom-call(bf16[256,128]{1,0:T(8,128)(2,1)S(1)} %get-tuple-element.25.grad_pre, bf16[128,256]{1,0:T(8,128)(2,1)S(1)} %get-tuple-element.26.first, bf16[256,256]{1,0:T(8,128)(2,1)S(1)} %get-tuple-element.27.lat_t), custom_call_target="tpu_custom_call" | custom-call | flops 37748736 | bytes 262144 | tf_op jit(solution)/shard_map/grad_lat/pallas_call | solution.py:379
  22.2 0.4 %collective-permute-done.1 = bf16[2,80,128]{2,1,0:T(8,128)(2,1)S(1)} collective-permute-done((bf16[2,80,128]{2,1,0:T(8,128)(2,1)S(1)}, bf16[2,80,128]{2,1,0:T(8,128)(2,1)S(1)}, u32[]{:S(2)}, u32[]{:S(2)}) %collective-permute-start.1) | collective-permute-done | bytes 40992 | tf_op jit(solution)/shard_map/ppermute | solution.py:400
  22.6 8.8 %all_to_all.11.pieces = bf16[8,104,128]{2,1,0:T(8,128)(2,1)S(1)} all-to-all(bf16[8,104,128]{2,1,0:T(8,128)(2,1)S(1)} %pad_maximum_fusion), channel_id=1, replica_groups=mesh['dp'=4,'space'=8] {'space'}, dimensions={0} | all-to-all | bytes 425984 | tf_op jit(solution)/shard_map/all_to_all | solution.py:403
  31.5 0.1 collective-permute-start.2
  31.5 1.5 %inverse_lon.1 = bf16[180,2,768]{2,1,0:T(2,128)(2,1)} custom-call(bf16[360,32]{1,0:T(8,128)(2,1)S(1)} %get-tuple-element.19.table, bf16[8,104,128]{2,1,0:T(8,128)(2,1)S(1)} %all_to_all.11.pieces), custom_call_target="tpu_custom_call" | custom-call | flops 17694720 | bytes 2211840 | tf_op jit(solution)/shard_map/inverse_lon/pallas_call | solution.py:413
  33.0 0.0 collective-permute-done.2.others
  33.0 0.9 %gathered.1 = (f32[2,192,96]{2,1,0:T(8,128)}, f32[2,192,96]{2,1,0:T(8,128)}, f32[2,192]{1,0:T(2,128)}, f32[2,192]{1,0:T(2,128)}) custom-call(bf16[8,104,128]{2,1,0:T(8,128)(2,1)S(1)} %all_to_all.11.pieces, bf16[8,80,128]{2,1,0:T(8,128)(2,1)S(1)} %collective-permute-done.2.others), custom_call_target="tpu_custom_call" | custom-call | tf_op jit(solution)/shard_map/gathered/pallas_call | solution.py:428
  (5 shorter events, 0.1 us)
Async XLA Ops:
  15.0 0.7 %collective-permute-start = (bf16[2,2,80,128]{3,2,1,0:T(8,128)(2,1)S(1)}, bf16[2,2,80,128]{3,2,1,0:T(8,128)(2,1)S(1)}, u32[]{:S(2)}, u32[]{:S(2)}) collective-permute-start(bf16[2,2,80,128]{3,2,1,0:T(8,128)(2,1)S(1)} %get-tuple-element.28), channel_id=1, source_target_pairs={{0,0},{1,9},{2,2},{3,11},{4,20},{5,29},{6,22},{7,31},{8,16},{9,25}... | collective-permute-start | bytes 245768 | tf_op jit(solution)/shard_map/ppermute | solution.py:391
  15.7 6.8 %collective-permute-start.1 = (bf16[2,80,128]{2,1,0:T(8,128)(2,1)S(1)}, bf16[2,80,128]{2,1,0:T(8,128)(2,1)S(1)}, u32[]{:S(2)}, u32[]{:S(2)}) collective-permute-start(bf16[2,80,128]{2,1,0:T(8,128)(2,1)S(1)} %slice_bitcast_fusion), channel_id=1, source_target_pairs={{0,1},{1,0},{2,3},{3,2},{4,5},{5,4},{6,7},{7,6},{8,9},{9,8},{10,11... | collective-permute-start | bytes 122888 | tf_op jit(solution)/shard_map/ppermute | solution.py:400
  31.5 1.5 %collective-permute-start.2 = (bf16[8,80,128]{2,1,0:T(8,128)(2,1)S(1)}, bf16[8,80,128]{2,1,0:T(8,128)(2,1)S(1)}, u32[]{:S(2)}, u32[]{:S(2)}) collective-permute-start(bf16[8,80,128]{2,1,0:T(8,128)(2,1)S(1)} %slice.14), channel_id=1, source_target_pairs={{0,1},{1,0},{2,3},{3,2},{4,5},{5,4},{6,7},{7,6},{8,9},{9,8},{10,11... | collective-permute-start | bytes 491528 | tf_op jit(solution)/shard_map/ppermute | solution.py:410
